TPU v7x, 32 devices: a whole 2x2x4 slice. The times are simulated.
32 devices in a mesh: parts: 2 (over y), shard: 2 (over core), blk: 8 (over z, x).
Axes of the slice: x: 2, y: 2, z: 4, core: 2. Of those that a mesh axis runs over, the one named last changes fastest.
Arguments:
- queries_in: bfloat16 [4096, 1024], P(('parts', 'shard', 'blk')), parts along dimension 0, may hold values from -12 to 12
- query_weight: bfloat16 [1024, 1024], replicated, may hold values from -0.1875 to 0.1875
- bank: bfloat16 [2048, 1024], P(('parts', 'shard', 'blk')), parts along dimension 0, may hold values from -110 to 110
- uses: int32 [4096, 2], P(('parts', 'shard', 'blk')), parts along dimension 0, may hold values from 0 to 1, as said below
Outputs:
- retrieved: bfloat16 [4096, 1024], P(('parts', 'shard', 'blk')), parts along dimension 0
There are 2 independent parts, one for each index of `parts`. A program takes and returns all parts, laid end to end along the dimension named above; an argument that names none is the same for every part. Nothing has to cross between parts.
Inputs may be any that keep to these rules, and one draw needn't show every extreme that they name: `uses`: every query lists one or both of the two shards. Of the 128 queries of one device, at most 128 list one shard, and in every draw for every index of blk the queries of both devices at that index all list one same shard.
All inputs are finite; a program needn't handle non-finite values.
Results may differ from a plain program's by a relative error of at most 0.035.
Values may be sent and summed in bfloat16 or wider, within the bound.
A program may use at most 128 MiB of HBM per device.

v0:
```python
import math
import jax
import jax.numpy as jnp
from jax import lax
from jax.sharding import PartitionSpec as P

HEADS = 8
HEAD_DIM = 128
NEGATIVE = -1e30


def empty_carry(slot_count):
    return (
        jnp.full((slot_count, HEADS), NEGATIVE, jnp.float32),
        jnp.zeros((slot_count, HEADS), jnp.float32),
        jnp.zeros((slot_count, HEADS, HEAD_DIM), jnp.float32),
    )


def fold_piece(carry, query_heads, piece, allowed):
    slot_count = query_heads.shape[0]
    piece_rows = piece.shape[0]
    key_rows = math.gcd(piece_rows, 512)
    key_blocks = piece_rows // key_rows
    keys_blocked = piece.reshape(key_blocks, key_rows, HEADS, HEAD_DIM)
    mask_blocked = allowed.reshape(slot_count, key_blocks, key_rows).transpose(1, 0, 2)
    block_rows = math.gcd(slot_count, 128)
    blocks = slot_count // block_rows
    logit_scale = HEAD_DIM ** (-0.5)

    def blocked(array):
        return array.reshape((blocks, block_rows) + array.shape[1:])

    def key_step(state, inputs):
        keys_piece, mask_all = inputs

        def one_block(block_inputs):
            query_block, mask_block, top_old, total_old, accum_old = block_inputs
            scores = (
                jnp.einsum(
                    "shd,rhd->shr", query_block, keys_piece, preferred_element_type=jnp.float32
                )
                * logit_scale
            )
            scores = jnp.where(mask_block[:, None, :], scores, NEGATIVE)
            top_new = jnp.maximum(top_old, jnp.max(scores, axis=-1))
            weights = jnp.where(mask_block[:, None, :], jnp.exp(scores - top_new[..., None]), 0.0)
            factor = jnp.exp(top_old - top_new)
            total_new = total_old * factor + jnp.sum(weights, axis=-1)
            accum_new = accum_old * factor[..., None] + jnp.einsum(
                "shr,rhd->shd",
                weights.astype(jnp.bfloat16),
                keys_piece,
                preferred_element_type=jnp.float32,
            )
            return (top_new, total_new, accum_new)

        top_old, total_old, accum_old = state
        results = lax.map(
            one_block,
            (
                blocked(query_heads),
                blocked(mask_all),
                blocked(top_old),
                blocked(total_old),
                blocked(accum_old),
            ),
        )
        return (
            tuple((result.reshape((slot_count,) + result.shape[2:]) for result in results)),
            None,
        )

    final, unused = lax.scan(key_step, carry, (keys_blocked, mask_blocked))
    return final


def local(queries_in, query_weight, bank, uses):
    row_count = queries_in.shape[0]
    width_all = HEADS * HEAD_DIM
    projected = jnp.dot(queries_in, query_weight, preferred_element_type=jnp.float32).astype(
        jnp.bfloat16
    )
    positions = jnp.cumsum(uses, axis=0) - 1
    listed = uses > 0
    onehot_table = (positions.T[:, None, :] == jnp.arange(row_count)[None, :, None]) & listed.T[
        :, None, :
    ]
    outgoing = jnp.einsum(
        "sct,td->scd",
        onehot_table.astype(jnp.bfloat16),
        projected,
        preferred_element_type=jnp.float32,
    ).astype(jnp.bfloat16)
    incoming = lax.all_to_all(outgoing, "shard", split_axis=0, concat_axis=0, tiled=True)
    item_count = incoming.shape[1]
    slot_heads = incoming.reshape(2 * item_count, HEADS, HEAD_DIM)
    piece = lax.all_gather(bank, "blk", axis=0, tiled=True)
    allowed = jnp.ones((2 * item_count, piece.shape[0]), dtype=jnp.bool_)
    top_part, total_part, accum_part = fold_piece(
        empty_carry(2 * item_count), slot_heads, piece, allowed
    )
    accum_back = lax.all_to_all(
        accum_part.reshape(2, item_count, width_all).astype(jnp.bfloat16),
        "shard",
        split_axis=0,
        concat_axis=0,
        tiled=True,
    ).astype(jnp.float32)
    top_back = lax.all_to_all(
        top_part.reshape(2, item_count, HEADS).astype(jnp.bfloat16),
        "shard",
        split_axis=0,
        concat_axis=0,
        tiled=True,
    ).astype(jnp.float32)
    total_back = lax.all_to_all(
        total_part.reshape(2, item_count, HEADS).astype(jnp.bfloat16),
        "shard",
        split_axis=0,
        concat_axis=0,
        tiled=True,
    ).astype(jnp.float32)
    safe_slot = jnp.clip(positions, 0, row_count - 1)
    top_pair = jnp.stack(
        [jnp.take(top_back[member], safe_slot[:, member], axis=0) for member in range(2)], 1
    )
    total_pair = jnp.stack(
        [jnp.take(total_back[member], safe_slot[:, member], axis=0) for member in range(2)], 1
    )
    accum_pair = jnp.stack(
        [jnp.take(accum_back[member], safe_slot[:, member], axis=0) for member in range(2)], 1
    )
    accum_pair = accum_pair.reshape(row_count, 2, HEADS, HEAD_DIM)
    top_pair = jnp.where(listed[:, :, None], top_pair, NEGATIVE)
    highest = jnp.max(top_pair, axis=1)
    scale_pair = jnp.where(listed[:, :, None], jnp.exp(top_pair - highest[:, None, :]), 0.0)
    total_all = jnp.sum(scale_pair * total_pair, axis=1)
    accum_all = jnp.sum(scale_pair[..., None] * accum_pair, axis=1)
    return (accum_all / total_all[..., None]).reshape(row_count, width_all).astype(jnp.bfloat16)


def solution(mesh):
    in_specs = (
        P(("parts", "shard", "blk"), None),
        P(),
        P(("parts", "shard", "blk"), None),
        P(("parts", "shard", "blk"), None),
    )
    out_specs = P(("parts", "shard", "blk"), None)
    return jax.shard_map(local, mesh=mesh, in_specs=in_specs, out_specs=out_specs, check_vma=False)
```

profile of v0, /device:TPU:1, one launch (start us, length us, event | category | flops | bytes accessed | tf_op | source)
XLA Modules:
  0.0 94.7 jit_solution(11347580435513448345)
XLA Ops:
  6.5 0.0 copy-start
  6.5 0.0 all-gather.2.cloned.1.call-start
  6.5 0.7 all-gather.2.cloned.1.call-update
  7.3 0.8 copy.41
  8.1 0.1 copy.45
  8.1 0.2 reduce_window_sum.11
  8.3 0.1 copy.44
  8.4 0.0 copy-done
  8.4 2.4 %convolution_convert_fusion = bf16[2,128,1024]{2,1,0:T(8,128)(2,1)} fusion(bf16[128,1024]{1,0:T(8,128)(2,1)} %param.10, bf16[1024,1024]{1,0:T(8,128)(2,1)S(1)} %copy-done, s32[2,128]{1,0:T(2,128)S(1)} %copy.44, pred[2,128]{1,0:T(4,128)(4,1)S(1)} %copy.45), kind=kOutput, calls=%fused_computation.29 | convolution fusion | flops 336003072 | bytes 2884864 | tf_op jit(solution)/shard_map/sct,td->scd/dot_general | solution.py:89
  10.8 3.5 %all-to-all-start = ((bf16[2,128,1024]{2,1,0:T(8,128)(2,1)}), bf16[2,128,1024]{2,1,0:T(8,128)(2,1)S(1)}, u32[]{:S(2)}, u32[]{:S(2)}) async-start(bf16[2,128,1024]{2,1,0:T(8,128)(2,1)} %convolution_convert_fusion), calls=%async_computation | async-start | bytes 1048576 | tf_op jit(solution)/shard_map/all_to_all | solution.py:95
  14.4 0.1 copy.42
  14.5 1.3 %all-to-all-done = bf16[2,128,1024]{2,1,0:T(8,128)(2,1)S(1)} async-done(((bf16[2,128,1024]{2,1,0:T(8,128)(2,1)}), bf16[2,128,1024]{2,1,0:T(8,128)(2,1)S(1)}, u32[]{:S(2)}, u32[]{:S(2)}) %all-to-all-start) | async-done | bytes 524320 | tf_op jit(solution)/shard_map/all_to_all | solution.py:95
  15.7 0.9 copy.60
  16.6 0.2 slice_reduce_fusion.1
  16.9 33.9 %all-gather.2.cloned.1.call-done = bf16[512,1024]{1,0:T(8,128)(2,1)} async-done(((bf16[64,1024]{1,0:T(8,128)(2,1)}), bf16[512,1024]{1,0:T(8,128)(2,1)}) %all-gather.2.cloned.1.call-update) | async-done | bytes 1048592 | tf_op jit(solution)/shard_map/all_gather | solution.py:98
  50.8 2.3 %copy.46 = bf16[512,1024]{0,1:T(8,128)(2,1)} copy(bf16[512,1024]{1,0:T(8,128)(2,1)} %all-gather.2.cloned.1.call-done) | data formatting | bytes 2097152 | tf_op jit(solution)/shard_map/all_gather | solution.py:98
  53.1 1.6 %copy.48 = bf16[512,8,128]{2,0,1:T(8,128)(2,1)S(1)} copy(bf16[512,8,128]{0,2,1:T(8,128)(2,1)} %bitcast.121) | data formatting | bytes 2097152 | tf_op jit(solution)/shard_map/while/body/eval_jaxpr/while | solution.py:59
  54.7 7.4 %while.26 = (s32[]{:T(128)}, bf16[2,128,8]{1,2,0:T(8,128)(2,1)S(1)}, bf16[2,128,8]{1,2,0:T(8,128)(2,1)}, bf16[2,128,8,128]{3,1,2,0:T(8,128)(2,1)}, bf16[2,128,8,...) while((s32[]{:T(128)}, bf16[2,128,8]{1,2,0:T(8,128)(2,1)S(1)}, ...), condition=%wide.region_4.5_spmd, body=%wide.region_1.4_spmd.sunk | while | flops 272768000 | bytes 13944989 | solution.py:59
  54.7 1.0 %constant_dynamic-slice_fusion.2 = bf16[1,128,8,128]{3,2,1,0:T(8,128)(2,1)S(1)} fusion(bf16[2,128,8,128]{3,2,1,0:T(8,128)(2,1)} %get-tuple-element.220, s32[]{:T(128)S(6)} %copy.80), kind=kLoop, calls=%fused_computation.27.clone.1 | loop fusion | bytes 524292 | tf_op jit(solution)/shard_map/while/body/eval_jaxpr/while/body/jit(dynamic_index_in_dim)/dynamic_slice | solution.py:59
  55.7 0.0 copy-start.2
  55.7 0.5 bitcast_reduce_fusion.2
  56.2 0.6 fusion.37
  56.8 0.0 copy-done.2
  56.8 0.7 fusion.39
  57.6 0.0 copy-start.3
  57.6 0.7 fusion.38
  58.2 0.1 copy-done.3
  58.4 1.0 %constant_dynamic-slice_fusion.2 = bf16[1,128,8,128]{3,2,1,0:T(8,128)(2,1)S(1)} fusion(bf16[2,128,8,128]{3,2,1,0:T(8,128)(2,1)} %get-tuple-element.220, s32[]{:T(128)S(6)} %copy.80), kind=kLoop, calls=%fused_computation.27.clone.1 | loop fusion | bytes 524292 | tf_op jit(solution)/shard_map/while/body/eval_jaxpr/while/body/jit(dynamic_index_in_dim)/dynamic_slice | solution.py:59
  59.4 0.0 copy-start.2
  59.4 0.5 bitcast_reduce_fusion.2
  59.9 0.6 fusion.37
  60.5 0.7 fusion.39
  61.3 0.7 fusion.38
  61.9 0.1 copy-done.3
  62.1 1.9 %copy_bitcast_fusion.2 = bf16[2,128,1024]{2,1,0:T(8,128)(2,1)} fusion(bf16[2,128,8,128]{3,1,2,0:T(8,128)(2,1)} %get-tuple-element.95), kind=kLoop, calls=%fused_computation.34 | loop fusion | bytes 1048576 | tf_op jit(solution)/shard_map/convert_element_type | solution.py:104
  64.0 5.0 %all_to_all.20 = bf16[2,128,8]{1,2,0:T(8,128)(2,1)S(1)} all-to-all(bf16[2,128,8]{1,2,0:T(8,128)(2,1)S(1)} %get-tuple-element.94), channel_id=1, replica_groups=mesh['parts'=2,'shard'=2,'blk'=8] {'shard'}, dimensions={0} | all-to-all | bytes 8192 | tf_op jit(solution)/shard_map/all_to_all | solution.py:110
  69.0 3.5 %all-to-all-start.3 = ((bf16[2,128,8]{1,2,0:T(8,128)(2,1)}), bf16[2,128,8]{1,2,0:T(8,128)(2,1)S(1)}, u32[]{:S(2)}, u32[]{:S(2)}) async-start(bf16[2,128,8]{1,2,0:T(8,128)(2,1)} %get-tuple-element.96), calls=%async_computation.3 | async-start | bytes 8192 | tf_op jit(solution)/shard_map/all_to_all | solution.py:117
  72.5 0.1 copy.49
  72.7 0.9 all-to-all-done.3
  73.6 3.8 %all-to-all-start.2 = ((bf16[2,128,1024]{2,1,0:T(8,128)(2,1)}), bf16[2,128,1024]{2,1,0:T(8,128)(2,1)S(1)}, u32[]{:S(2)}, u32[]{:S(2)}) async-start(bf16[2,128,1024]{2,1,0:T(8,128)(2,1)} %copy_bitcast_fusion.2), calls=%async_computation.2 | async-start | bytes 1048576 | tf_op jit(solution)/shard_map/all_to_all | solution.py:103
  77.4 0.1 copy.54
  77.5 0.6 gather_fusion
  78.2 0.6 gather_fusion.4
  78.8 0.1 select_bitcast_fusion.5
  79.0 0.1 copy.55
  79.0 0.7 gather_fusion.1
  79.7 0.6 gather_fusion.5
  80.4 0.1 select_bitcast_fusion.4
  80.5 0.1 copy.56
  80.6 0.1 copy.57
  80.7 0.1 copy.52
  80.8 0.0 all-to-all-done.2
  80.9 0.1 convert_element_type.45
  81.0 0.1 slice_bitcast_fusion.1
  81.0 1.6 %gather_fusion.2 = f32[128,1024]{1,0:T(8,128)} fusion(f32[128,1024]{1,0:T(8,128)S(1)} %get-tuple-element.141, s32[1024]{0:T(1024)S(1)} %pad_clamp_fusion.1), kind=kCustom, calls=%fused_computation.1.clone | custom fusion | bytes 1049088 | tf_op jit(solution)/shard_map/jit(_take)/gather | solution.py:132
  82.6 1.1 %select_bitcast_fusion.1 = f32[16,8,8,128]{3,1,2,0:T(8,128)S(1)} fusion(f32[128,1024]{1,0:T(8,128)} %gather_fusion.2, pred[128]{0:T(512)(128)(4,1)S(1)} %get-tuple-element.156), kind=kLoop, calls=%fused_computation.38 | loop fusion | flops 131072 | bytes 1048704
  83.8 0.9 copy.61
  84.7 0.8 gather_fusion.3
  85.5 0.1 select_bitcast_fusion
  85.6 0.1 copy.62
  85.7 0.8 copy-done.1
  86.5 0.3 fusion.15
  86.8 0.2 divide_convert_fusion
  87.1 0.8 copy.70
  (25 shorter events, 0.3 us)
Async XLA Ops:
  6.5 1.9 %copy-start = (bf16[1024,1024]{1,0:T(8,128)(2,1)S(1)}, bf16[1024,1024]{1,0:T(8,128)(2,1)}, u32[]{:S(2)}) copy-start(bf16[1024,1024]{1,0:T(8,128)(2,1)} %param.11) | copy-start | bytes 6291460
  6.5 44.3 %all-gather.2.cloned.1.call-start = ((), (), s32[]{:S(2)}) async-start(), calls=%async_computation.4 | async-start | bytes 1179648 | tf_op jit(solution)/shard_map/all_gather | solution.py:98
  10.8 4.9 %all-to-all-start = ((bf16[2,128,1024]{2,1,0:T(8,128)(2,1)}), bf16[2,128,1024]{2,1,0:T(8,128)(2,1)S(1)}, u32[]{:S(2)}, u32[]{:S(2)}) async-start(bf16[2,128,1024]{2,1,0:T(8,128)(2,1)} %convolution_convert_fusion), calls=%async_computation | async-start | bytes 1048576 | tf_op jit(solution)/shard_map/all_to_all | solution.py:95
  55.7 1.1 %copy-start.2 = (bf16[2,128,8,128]{3,1,2,0:T(8,128)(2,1)S(1)}, bf16[2,128,8,128]{3,1,2,0:T(8,128)(2,1)}, u32[]{:S(2)}) copy-start(bf16[2,128,8,128]{3,1,2,0:T(8,128)(2,1)} %get-tuple-element.212) | copy-start | bytes 1572868 | tf_op jit(solution)/shard_map/while/body/eval_jaxpr/while
  57.6 0.8 copy-start.3
  59.4 1.1 %copy-start.2 = (bf16[2,128,8,128]{3,1,2,0:T(8,128)(2,1)S(1)}, bf16[2,128,8,128]{3,1,2,0:T(8,128)(2,1)}, u32[]{:S(2)}) copy-start(bf16[2,128,8,128]{3,1,2,0:T(8,128)(2,1)} %get-tuple-element.212) | copy-start | bytes 1572868 | tf_op jit(solution)/shard_map/while/body/eval_jaxpr/while
  61.3 0.8 copy-start.3
  69.0 4.6 %all-to-all-start.3 = ((bf16[2,128,8]{1,2,0:T(8,128)(2,1)}), bf16[2,128,8]{1,2,0:T(8,128)(2,1)S(1)}, u32[]{:S(2)}, u32[]{:S(2)}) async-start(bf16[2,128,8]{1,2,0:T(8,128)(2,1)} %get-tuple-element.96), calls=%async_computation.3 | async-start | bytes 8192 | tf_op jit(solution)/shard_map/all_to_all | solution.py:117
  73.6 7.3 %all-to-all-start.2 = ((bf16[2,128,1024]{2,1,0:T(8,128)(2,1)}), bf16[2,128,1024]{2,1,0:T(8,128)(2,1)S(1)}, u32[]{:S(2)}, u32[]{:S(2)}) async-start(bf16[2,128,1024]{2,1,0:T(8,128)(2,1)} %copy_bitcast_fusion.2), calls=%async_computation.2 | async-start | bytes 1048576 | tf_op jit(solution)/shard_map/all_to_all | solution.py:103
  85.5 1.0 %copy-start.1 = (f32[16,8,8,128]{3,2,1,0:T(8,128)S(1)}, f32[16,8,8,128]{3,2,1,0:T(8,128)}, u32[]{:S(2)}) copy-start(f32[16,8,8,128]{3,2,1,0:T(8,128)} %copy.61) | copy-start | bytes 1572868
Sparse Core Ops, SparseCore 0:
  9.5 41.2 all-gather.1
where the time goes:
time: 95.3 us; the launch traced here: 94.7 us
  waiting for transfers between devices  36.8 us (39%)
  local copies, waits for them, and re-layouts  18.4 us (19%)
  between operations  13.6 us (14%)
  starting transfers between devices  10.9 us (11%)
  blocking collectives  5.01 us (5%)
  matrix products  4.94 us (5%)
  other arithmetic  4.87 us (5%)
    all_gather x1, waiting for transfers between devices, local(): piece = lax.all_gather(bank, 'blk', axis=0, tiled=True)  33.9 us
    all_to_all x1, blocking collectives, local(): lax.all_to_all(top_part.reshape(2, item_count, HEADS).astype(jnp.bfloat16...  5.01 us
    unnamed x9, local copies, waits for them, and re-layouts  4.23 us
    all_to_all x1, starting transfers between devices, local(): lax.all_to_all(accum_part.reshape(2, item_count, width_all).astype(jnp.bf...  3.81 us
    all_to_all x1, starting transfers between devices, local(): lax.all_to_all(total_part.reshape(2, item_count, HEADS).astype(jnp.bfloat...  3.55 us
    all_to_all x1, starting transfers between devices, local(): lax.all_to_all(outgoing, 'shard', split_axis=0, concat_axis=0, tiled=True)  3.53 us
    dot_general x1, matrix products, local(): jnp.einsum('sct,td->scd', onehot_table.astype(jnp.bfloat16), projected, p...  2.43 us
    gather x2, local copies, waits for them, and re-layouts, local(): jnp.take(accum_back[member], safe_slot[:, member], axis=0)  2.38 us
  transfers between devices with their start and end apart: 4, of which 3 were waited for; matrix products, arithmetic and copies ran while one was open for 9% of the time, Pallas kernels for 0%

commit v1 on v0

--- a/solution.py
+++ b/solution.py
@@ -1,3 +1,4 @@
+import functools
 import math
 import jax
 import jax.numpy as jnp
@@ -7,6 +8,27 @@
 HEADS = 8
 HEAD_DIM = 128
 NEGATIVE = -1e30
+
+
+def convert_the_records(sample, out_dim):
+    shares = lax.axis_size("blk")
+    tmp = range(shares)
+    passed = map(lambda kk: (kk, (kk + 1) % shares), tmp)
+    rack = list(passed)
+
+    def use_teams_in(val2):
+        if len(val2) == shares:
+            return val2
+        small = lax.ppermute(val2[0], "blk", rack)
+        return use_teams_in([small, *val2])
+
+    block_now = use_teams_in([sample])
+    finding = jnp.concatenate(block_now, axis=out_dim)
+    view_out = lax.axis_index("blk")
+    return jnp.roll(finding, (view_out + 1) * sample.shape[out_dim], axis=out_dim)
+
+
+pools_keep_up = functools.partial(convert_the_records, out_dim=0)
 
 
 def empty_carry(slot_count):
@@ -95,7 +117,7 @@
     incoming = lax.all_to_all(outgoing, "shard", split_axis=0, concat_axis=0, tiled=True)
     item_count = incoming.shape[1]
     slot_heads = incoming.reshape(2 * item_count, HEADS, HEAD_DIM)
-    piece = lax.all_gather(bank, "blk", axis=0, tiled=True)
+    piece = pools_keep_up(bank)
     allowed = jnp.ones((2 * item_count, piece.shape[0]), dtype=jnp.bool_)
     top_part, total_part, accum_part = fold_piece(
         empty_carry(2 * item_count), slot_heads, piece, allowed

time: 95.3 us -> 115 us (1.21)
  between operations: 13.6 us -> 0.24 us
  waiting for transfers between devices: 36.8 us -> 49.9 us
  local copies, waits for them, and re-layouts: 18.4 us -> 27.6 us
  blocking collectives: 5.01 us -> 10.9 us
  starting transfers between devices: 10.9 us -> 15.1 us
    ppermute x0 -> x7, waiting for transfers between devices: none -> 49 us  [use_teams_in(): small = lax.ppermute(val2[0], 'blk', rack)]
    all_gather x1 -> x0, waiting for transfers between devices: 33.9 us -> none  [local(): piece = lax.all_gather(bank, 'blk', axis=0, tiled=True)]
    concatenate x0 -> x1, local copies, waits for them, and re-layouts: none -> 5.97 us  [convert_the_records(): jnp.roll(finding, (view_out + 1) * sample.shape[out_dim], axis=out_dim)]
    all_to_all x1, blocking collectives: 5.01 us -> 10.9 us  [local(): lax.all_to_all(top_part.reshape(2, item_count, HEADS).astype(jnp.bfloat16...]
    dynamic_slice x0 -> x1, local copies, waits for them, and re-layouts: none -> 2.77 us  [convert_the_records(): jnp.roll(finding, (view_out + 1) * sample.shape[out_dim], axis=out_dim)]
    unnamed x9 -> x14, local copies, waits for them, and re-layouts: 4.23 us -> 6.91 us
    all_gather x1 -> x0, local copies, waits for them, and re-layouts: 2.28 us -> none  [local(): piece = lax.all_gather(bank, 'blk', axis=0, tiled=True)]
    ppermute x0 -> x7, starting transfers between devices: none -> 2.11 us  [use_teams_in(): small = lax.ppermute(val2[0], 'blk', rack)]
  transfers between devices with their start and end apart: 4 -> 10, of which waited for: 3 -> 8; matrix products, arithmetic and copies ran while one was open for 9% -> 7% of each run, Pallas kernels for 0% -> 0%
where the time goes in v1:
time: 115 us; the launch traced here: 114 us
  waiting for transfers between devices  49.9 us (43%)
  local copies, waits for them, and re-layouts  27.6 us (24%)
  starting transfers between devices  15.1 us (13%)
  blocking collectives  10.9 us (9%)
  matrix products  4.98 us (4%)
  other arithmetic  4.85 us (4%)
    ppermute x7, waiting for transfers between devices, use_teams_in(): small = lax.ppermute(val2[0], 'blk', rack)  49 us
    all_to_all x1, blocking collectives, local(): lax.all_to_all(top_part.reshape(2, item_count, HEADS).astype(jnp.bfloat16...  10.9 us
    unnamed x14, local copies, waits for them, and re-layouts  6.91 us
    concatenate x1, local copies, waits for them, and re-layouts, convert_the_records(): jnp.roll(finding, (view_out + 1) * sample.shape[out_dim], axis=out_dim)  5.97 us
    all_to_all x1, starting transfers between devices, local(): lax.all_to_all(outgoing, 'shard', split_axis=0, concat_axis=0, tiled=True)  5.62 us
    all_to_all x1, starting transfers between devices, local(): lax.all_to_all(accum_part.reshape(2, item_count, width_all).astype(jnp.bf...  3.81 us
    all_to_all x1, starting transfers between devices, local(): lax.all_to_all(total_part.reshape(2, item_count, HEADS).astype(jnp.bfloat...  3.52 us
    dynamic_slice x1, local copies, waits for them, and re-layouts, convert_the_records(): jnp.roll(finding, (view_out + 1) * sample.shape[out_dim], axis=out_dim)  2.77 us
  transfers between devices with their start and end apart: 10, of which 8 were waited for; matrix products, arithmetic and copies ran while one was open for 7% of the time, Pallas kernels for 0%

profile of v1, /device:TPU:1, one launch (start us, length us, event | category | flops | bytes accessed | tf_op | source)
XLA Modules:
  0.0 113.7 jit_solution(7580701990203605243)
XLA Ops:
  0.0 1.2 %copy.50 = bf16[64,1024]{0,1:T(8,128)(2,1)S(1)} copy(bf16[64,1024]{1,0:T(8,128)(2,1)} %param.12) | data formatting | bytes 262144 | tf_op args[2]
  1.2 2.1 %collective-permute-start = (bf16[64,1024]{0,1:T(8,128)(2,1)S(1)}, bf16[64,1024]{0,1:T(8,128)(2,1)S(1)}, u32[]{:S(2)}, u32[]{:S(2)}) collective-permute-start(bf16[64,1024]{0,1:T(8,128)(2,1)S(1)} %copy.50), channel_id=1, source_target_pairs={{0,1},{1,2},{2,3},{3,4},{4,5},{5,6},{6,7},{7,0},{8,9},{9,10},{10,1... | collective-permute-start | bytes 393224 | tf_op jit(solution)/shard_map/ppermute | solution.py:22
  3.3 0.8 copy.45
  4.1 0.1 copy.49
  4.2 0.2 reduce_window_sum.11
  4.4 8.0 %collective-permute-done = bf16[64,1024]{0,1:T(8,128)(2,1)S(1)} collective-permute-done((bf16[64,1024]{0,1:T(8,128)(2,1)S(1)}, bf16[64,1024]{0,1:T(8,128)(2,1)S(1)}, u32[]{:S(2)}, u32[]{:S(2)}) %collective-permute-start) | collective-permute-done | bytes 131104 | tf_op jit(solution)/shard_map/ppermute | solution.py:22
  12.5 9.2 %collective-permute-done.1 = bf16[64,1024]{0,1:T(8,128)(2,1)S(1)} collective-permute-done((bf16[64,1024]{0,1:T(8,128)(2,1)S(1)}, bf16[64,1024]{0,1:T(8,128)(2,1)S(1)}, u32[]{:S(2)}, u32[]{:S(2)}) %collective-permute-start.1) | collective-permute-done | bytes 131104 | tf_op jit(solution)/shard_map/ppermute | solution.py:22
  21.7 2.4 %convolution_convert_fusion = bf16[2,128,1024]{2,1,0:T(8,128)(2,1)} fusion(bf16[128,1024]{1,0:T(8,128)(2,1)} %param.10, bf16[1024,1024]{1,0:T(8,128)(2,1)S(1)} %copy-done, s32[2,128]{1,0:T(2,128)S(1)} %copy.48, pred[2,128]{1,0:T(4,128)(4,1)S(1)} %copy.49), kind=kOutput, calls=%fused_computation.29 | convolution fusion | flops 336003072 | bytes 2884864 | tf_op jit(solution)/shard_map/sct,td->scd/dot_general | solution.py:111
  24.1 5.6 %all-to-all-start = ((bf16[2,128,1024]{2,1,0:T(8,128)(2,1)}), bf16[2,128,1024]{2,1,0:T(8,128)(2,1)S(1)}, u32[]{:S(2)}, u32[]{:S(2)}) async-start(bf16[2,128,1024]{2,1,0:T(8,128)(2,1)} %convolution_convert_fusion), calls=%async_computation | async-start | bytes 1048576 | tf_op jit(solution)/shard_map/all_to_all | solution.py:117
  29.7 0.4 collective-permute-done.2
  30.1 0.2 slice_reduce_fusion.1
  30.3 7.9 %collective-permute-done.3 = bf16[64,1024]{0,1:T(8,128)(2,1)S(1)} collective-permute-done((bf16[64,1024]{0,1:T(8,128)(2,1)}, bf16[64,1024]{0,1:T(8,128)(2,1)S(1)}, u32[]{:S(2)}, u32[]{:S(2)}) %collective-permute-start.3) | collective-permute-done | bytes 131104 | tf_op jit(solution)/shard_map/ppermute | solution.py:22
  38.2 0.7 copy-done.2
  39.0 7.9 %collective-permute-done.4 = bf16[64,1024]{0,1:T(8,128)(2,1)S(1)} collective-permute-done((bf16[64,1024]{0,1:T(8,128)(2,1)S(1)}, bf16[64,1024]{0,1:T(8,128)(2,1)S(1)}, u32[]{:S(2)}, u32[]{:S(2)}) %collective-permute-start.4) | collective-permute-done | bytes 131104 | tf_op jit(solution)/shard_map/ppermute | solution.py:22
  46.9 0.7 copy-done.3
  47.6 8.0 %collective-permute-done.5 = bf16[64,1024]{0,1:T(8,128)(2,1)} collective-permute-done((bf16[64,1024]{0,1:T(8,128)(2,1)S(1)}, bf16[64,1024]{0,1:T(8,128)(2,1)}, u32[]{:S(2)}, u32[]{:S(2)}) %collective-permute-start.5) | collective-permute-done | bytes 131104 | tf_op jit(solution)/shard_map/ppermute | solution.py:22
  55.7 0.1 copy.46
  55.8 0.9 copy.66
  56.7 7.6 %collective-permute-done.6 = bf16[64,1024]{0,1:T(8,128)(2,1)} collective-permute-done((bf16[64,1024]{0,1:T(8,128)(2,1)}, bf16[64,1024]{0,1:T(8,128)(2,1)}, u32[]{:S(2)}, u32[]{:S(2)}) %collective-permute-start.6) | collective-permute-done | bytes 131104 | tf_op jit(solution)/shard_map/ppermute | solution.py:22
  64.2 6.0 %concatenate.11 = bf16[1024,1024]{0,1:T(8,128)(2,1)} concatenate(bf16[64,1024]{0,1:T(8,128)(2,1)} %collective-permute-done.6, bf16[64,1024]{0,1:T(8,128)(2,1)} %collective-permute-done.5, bf16[64,1024]{0,1:T(8,128)(2,1)} %copy-done.3, bf16[64,1024]{0,1:T(8,128)(2,1)} %copy-done.2, bf16[64,1024]{0,1:T(8,128)(2,1)} %collective-permute-done.2, ...), dimensions={0} | concatenate | bytes 4194304 | tf_op jit(solution)/shard_map/jit(_roll_dynamic)/concatenate | solution.py:28
  70.2 2.8 %constant_dynamic-slice_fusion.1 = bf16[512,1024]{0,1:T(8,128)(2,1)} fusion(bf16[1024,1024]{0,1:T(8,128)(2,1)} %concatenate.11, s32[]{:T(128)S(6)} %select_n.49), kind=kLoop, calls=%fused_computation.70 | loop fusion | bytes 2097156 | tf_op jit(solution)/shard_map/jit(_roll_dynamic)/dynamic_slice | solution.py:28
  73.0 1.6 %copy.54 = bf16[512,8,128]{2,0,1:T(8,128)(2,1)S(1)} copy(bf16[512,8,128]{0,2,1:T(8,128)(2,1)} %bitcast.121) | data formatting | bytes 2097152 | tf_op jit(solution)/shard_map/while/body/eval_jaxpr/while | solution.py:81
  74.6 7.4 %while.26 = (s32[]{:T(128)}, bf16[2,128,8]{1,2,0:T(8,128)(2,1)S(1)}, bf16[2,128,8]{1,2,0:T(8,128)(2,1)}, bf16[2,128,8,128]{3,1,2,0:T(8,128)(2,1)}, bf16[2,128,8,...) while((s32[]{:T(128)}, bf16[2,128,8]{1,2,0:T(8,128)(2,1)S(1)}, ...), condition=%wide.region_4.5_spmd, body=%wide.region_1.4_spmd.sunk | while | flops 272768000 | bytes 13944989 | solution.py:81
  74.6 1.0 constant_dynamic-slice_fusion.3
  75.6 0.5 bitcast_reduce_fusion.2
  76.1 0.6 fusion.37
  76.7 0.8 fusion.39
  77.5 0.6 fusion.38
  78.2 0.2 copy-done.5
  78.3 1.0 constant_dynamic-slice_fusion.3
  79.3 0.5 bitcast_reduce_fusion.2
  79.8 0.6 fusion.37
  80.5 0.8 fusion.39
  81.2 0.6 fusion.38
  81.9 0.1 copy-done.5
  82.0 1.9 %copy_bitcast_fusion.2 = bf16[2,128,1024]{2,1,0:T(8,128)(2,1)} fusion(bf16[2,128,8,128]{3,1,2,0:T(8,128)(2,1)} %get-tuple-element.95), kind=kLoop, calls=%fused_computation.34 | loop fusion | bytes 1048576 | tf_op jit(solution)/shard_map/convert_element_type | solution.py:126
  84.0 10.9 %all_to_all.20 = bf16[2,128,8]{1,2,0:T(8,128)(2,1)S(1)} all-to-all(bf16[2,128,8]{1,2,0:T(8,128)(2,1)S(1)} %get-tuple-element.94), channel_id=1, replica_groups=mesh['parts'=2,'shard'=2,'blk'=8] {'shard'}, dimensions={0} | all-to-all | bytes 8192 | tf_op jit(solution)/shard_map/all_to_all | solution.py:132
  94.9 3.5 %all-to-all-start.3 = ((bf16[2,128,8]{1,2,0:T(8,128)(2,1)}), bf16[2,128,8]{1,2,0:T(8,128)(2,1)S(1)}, u32[]{:S(2)}, u32[]{:S(2)}) async-start(bf16[2,128,8]{1,2,0:T(8,128)(2,1)} %get-tuple-element.96), calls=%async_computation.3 | async-start | bytes 8192 | tf_op jit(solution)/shard_map/all_to_all | solution.py:139
  98.4 0.1 copy.55
  98.6 0.9 all-to-all-done.3
  99.5 3.8 %all-to-all-start.2 = ((bf16[2,128,1024]{2,1,0:T(8,128)(2,1)}), bf16[2,128,1024]{2,1,0:T(8,128)(2,1)S(1)}, u32[]{:S(2)}, u32[]{:S(2)}) async-start(bf16[2,128,1024]{2,1,0:T(8,128)(2,1)} %copy_bitcast_fusion.2), calls=%async_computation.2 | async-start | bytes 1048576 | tf_op jit(solution)/shard_map/all_to_all | solution.py:125
  103.3 0.1 copy.60
  103.4 0.6 gather_fusion
  104.1 0.6 gather_fusion.4
  104.7 0.1 select_bitcast_fusion.5
  104.9 0.1 copy.61
  104.9 0.7 gather_fusion.1
  105.6 0.6 gather_fusion.5
  106.2 0.1 select_bitcast_fusion.4
  106.4 0.1 copy.62
  106.5 0.1 copy.63
  106.6 0.1 copy.58
  106.7 0.1 convert_element_type.45
  106.8 0.1 slice_bitcast_fusion.1
  106.9 1.6 %gather_fusion.2 = f32[128,1024]{1,0:T(8,128)} fusion(f32[128,1024]{1,0:T(8,128)S(1)} %get-tuple-element.141, s32[1024]{0:T(1024)S(1)} %pad_clamp_fusion.1), kind=kCustom, calls=%fused_computation.1.clone | custom fusion | bytes 1049088 | tf_op jit(solution)/shard_map/jit(_take)/gather | solution.py:154
  108.5 1.1 %select_bitcast_fusion.1 = f32[16,8,8,128]{3,1,2,0:T(8,128)S(1)} fusion(f32[128,1024]{1,0:T(8,128)} %gather_fusion.2, pred[128]{0:T(512)(128)(4,1)S(1)} %get-tuple-element.156), kind=kLoop, calls=%fused_computation.38 | loop fusion | flops 131072 | bytes 1048704
  109.7 0.9 copy.67
  110.6 0.8 gather_fusion.3
  111.4 0.1 select_bitcast_fusion
  111.5 0.1 copy.68
  111.6 0.8 copy-done.1
  112.4 0.3 fusion.15
  112.7 0.2 divide_convert_fusion
  113.0 0.8 copy.76
  (42 shorter events, 0.4 us)
Async XLA Ops:
  0.0 21.7 %copy-start = (bf16[1024,1024]{1,0:T(8,128)(2,1)S(1)}, bf16[1024,1024]{1,0:T(8,128)(2,1)}, u32[]{:S(2)}) copy-start(bf16[1024,1024]{1,0:T(8,128)(2,1)} %param.11) | copy-start | bytes 6291460
  1.2 11.2 %collective-permute-start = (bf16[64,1024]{0,1:T(8,128)(2,1)S(1)}, bf16[64,1024]{0,1:T(8,128)(2,1)S(1)}, u32[]{:S(2)}, u32[]{:S(2)}) collective-permute-start(bf16[64,1024]{0,1:T(8,128)(2,1)S(1)} %copy.50), channel_id=1, source_target_pairs={{0,1},{1,2},{2,3},{3,4},{4,5},{5,6},{6,7},{7,0},{8,9},{9,10},{10,1... | collective-permute-start | bytes 393224 | tf_op jit(solution)/shard_map/ppermute | solution.py:22
  12.4 9.3 %collective-permute-start.1 = (bf16[64,1024]{0,1:T(8,128)(2,1)S(1)}, bf16[64,1024]{0,1:T(8,128)(2,1)S(1)}, u32[]{:S(2)}, u32[]{:S(2)}) collective-permute-start(bf16[64,1024]{0,1:T(8,128)(2,1)S(1)} %collective-permute-done), channel_id=1, source_target_pairs={{0,1},{1,2},{2,3},{3,4},{4,5},{5,6},{6,7},{7,0},{8,9},{9,10},{10,1... | collective-permute-start | bytes 393224 | tf_op jit(solution)/shard_map/ppermute | solution.py:22
  21.7 8.5 %collective-permute-start.2 = (bf16[64,1024]{0,1:T(8,128)(2,1)S(1)}, bf16[64,1024]{0,1:T(8,128)(2,1)}, u32[]{:S(2)}, u32[]{:S(2)}) collective-permute-start(bf16[64,1024]{0,1:T(8,128)(2,1)S(1)} %collective-permute-done.1), channel_id=1, source_target_pairs={{0,1},{1,2},{2,3},{3,4},{4,5},{5,6},{6,7},{7,0},{8,9},{9,10},{10,1... | collective-permute-start | bytes 393224 | tf_op jit(solution)/shard_map/ppermute | solution.py:22
  24.1 31.7 %all-to-all-start = ((bf16[2,128,1024]{2,1,0:T(8,128)(2,1)}), bf16[2,128,1024]{2,1,0:T(8,128)(2,1)S(1)}, u32[]{:S(2)}, u32[]{:S(2)}) async-start(bf16[2,128,1024]{2,1,0:T(8,128)(2,1)} %convolution_convert_fusion), calls=%async_computation | async-start | bytes 1048576 | tf_op jit(solution)/shard_map/all_to_all | solution.py:117
  30.1 8.1 %collective-permute-start.3 = (bf16[64,1024]{0,1:T(8,128)(2,1)}, bf16[64,1024]{0,1:T(8,128)(2,1)S(1)}, u32[]{:S(2)}, u32[]{:S(2)}) collective-permute-start(bf16[64,1024]{0,1:T(8,128)(2,1)} %collective-permute-done.2), channel_id=1, source_target_pairs={{0,1},{1,2},{2,3},{3,4},{4,5},{5,6},{6,7},{7,0},{8,9},{9,10},{10,1... | collective-permute-start | bytes 393224 | tf_op jit(solution)/shard_map/ppermute | solution.py:22
  38.2 0.7 copy-start.2
  39.0 7.9 %collective-permute-start.4 = (bf16[64,1024]{0,1:T(8,128)(2,1)S(1)}, bf16[64,1024]{0,1:T(8,128)(2,1)S(1)}, u32[]{:S(2)}, u32[]{:S(2)}) collective-permute-start(bf16[64,1024]{0,1:T(8,128)(2,1)S(1)} %collective-permute-done.3), channel_id=1, source_target_pairs={{0,1},{1,2},{2,3},{3,4},{4,5},{5,6},{6,7},{7,0},{8,9},{9,10},{10,1... | collective-permute-start | bytes 393224 | tf_op jit(solution)/shard_map/ppermute | solution.py:22
  46.9 0.7 copy-start.3
  47.6 8.0 %collective-permute-start.5 = (bf16[64,1024]{0,1:T(8,128)(2,1)S(1)}, bf16[64,1024]{0,1:T(8,128)(2,1)}, u32[]{:S(2)}, u32[]{:S(2)}) collective-permute-start(bf16[64,1024]{0,1:T(8,128)(2,1)S(1)} %collective-permute-done.4), channel_id=1, source_target_pairs={{0,1},{1,2},{2,3},{3,4},{4,5},{5,6},{6,7},{7,0},{8,9},{9,10},{10,1... | collective-permute-start | bytes 393224 | tf_op jit(solution)/shard_map/ppermute | solution.py:22
  55.6 8.6 %collective-permute-start.6 = (bf16[64,1024]{0,1:T(8,128)(2,1)}, bf16[64,1024]{0,1:T(8,128)(2,1)}, u32[]{:S(2)}, u32[]{:S(2)}) collective-permute-start(bf16[64,1024]{0,1:T(8,128)(2,1)} %collective-permute-done.5), channel_id=1, source_target_pairs={{0,1},{1,2},{2,3},{3,4},{4,5},{5,6},{6,7},{7,0},{8,9},{9,10},{10,1... | collective-permute-start | bytes 393224 | tf_op jit(solution)/shard_map/ppermute | solution.py:22
  75.6 1.1 %copy-start.4 = (bf16[2,128,8,128]{3,1,2,0:T(8,128)(2,1)S(1)}, bf16[2,128,8,128]{3,1,2,0:T(8,128)(2,1)}, u32[]{:S(2)}) copy-start(bf16[2,128,8,128]{3,1,2,0:T(8,128)(2,1)} %get-tuple-element.212) | copy-start | bytes 1572868 | tf_op jit(solution)/shard_map/while/body/eval_jaxpr/while
  77.5 0.8 copy-start.5
  79.3 1.1 %copy-start.4 = (bf16[2,128,8,128]{3,1,2,0:T(8,128)(2,1)S(1)}, bf16[2,128,8,128]{3,1,2,0:T(8,128)(2,1)}, u32[]{:S(2)}) copy-start(bf16[2,128,8,128]{3,1,2,0:T(8,128)(2,1)} %get-tuple-element.212) | copy-start | bytes 1572868 | tf_op jit(solution)/shard_map/while/body/eval_jaxpr/while
  81.2 0.8 copy-start.5
  94.9 4.5 %all-to-all-start.3 = ((bf16[2,128,8]{1,2,0:T(8,128)(2,1)}), bf16[2,128,8]{1,2,0:T(8,128)(2,1)S(1)}, u32[]{:S(2)}, u32[]{:S(2)}) async-start(bf16[2,128,8]{1,2,0:T(8,128)(2,1)} %get-tuple-element.96), calls=%async_computation.3 | async-start | bytes 8192 | tf_op jit(solution)/shard_map/all_to_all | solution.py:139
  99.5 7.3 %all-to-all-start.2 = ((bf16[2,128,1024]{2,1,0:T(8,128)(2,1)}), bf16[2,128,1024]{2,1,0:T(8,128)(2,1)S(1)}, u32[]{:S(2)}, u32[]{:S(2)}) async-start(bf16[2,128,1024]{2,1,0:T(8,128)(2,1)} %copy_bitcast_fusion.2), calls=%async_computation.2 | async-start | bytes 1048576 | tf_op jit(solution)/shard_map/all_to_all | solution.py:125
  111.4 1.0 copy-start.1
